TPU v7x, 256 devices: a whole 4x4x8 slice. The times are simulated.
256 devices in a mesh: grp: 16 (over y, z_lo), tp: 16 (over z_hi, x, core).
Axes of the slice: x: 4, y: 4, z: 8 (z_hi: 2, z_lo: 4; z = z_hi * 4 + z_lo), core: 2. Of those that a mesh axis runs over, the one named last changes fastest.
Arguments:
- pre_act: bfloat16 [16, 2048, 4096], P('grp', None, 'tp'), may hold values from -6 to 6
- cotangent: bfloat16 [16, 2048, 2048], P('grp', 'tp'), may hold values from -6 to 6
- w_down: bfloat16 [16, 4096, 2048], P('grp', 'tp'), may hold values from -0.09375 to 0.09375
- first_moment: float32 [16, 4096, 2048], P('grp', 'tp'), may hold values from -4 to 4
- second_moment: float32 [16, 4096, 2048], P('grp', 'tp'), may hold values from 0.05 to 2
- path_table: int32 [16], replicated, may hold values from 0 to 15, as said below
- sharer_counts: int32 [16], replicated, may hold values from 0 to 8, as said below
Outputs:
- grad_avg: bfloat16 [16, 4096, 2048], P('grp', 'tp')
- first_avg: float32 [16, 4096, 2048], P('grp', 'tp')
- second_avg: float32 [16, 4096, 2048], P('grp', 'tp')
- pre_grad: bfloat16 [16, 2048, 4096], P('grp', None, 'tp')
Inputs may be any that keep to these rules, and one draw needn't show every extreme that they name: `path_table`: exactly 8 groups have module 16 - 1 and exactly one group has module 0. `sharer_counts`: entry m is the number of entries of path_table equal to m.
All inputs are finite; a program needn't handle non-finite values.
Results may differ from a plain program's by a relative error of at most 0.0051.
Values may be sent and summed in bfloat16 or wider, within the bound.
A program may use at most 128 MiB of HBM per device.

v0:
```python
import math

import jax
import jax.numpy as jnp
from jax import lax
from jax.sharding import PartitionSpec as P


def blend_rows(sharing, pieces):
    return tuple(
        (
            jnp.einsum("gh,hrc->grc", sharing, member, precision=lax.Precision.HIGHEST)
            for member in pieces
        )
    )


def per_device(pre_act, cotangent, w_down, first_moment, second_moment, path_table, sharer_counts):
    inv_root_two = 1.0 / math.sqrt(2.0)
    inv_root_tau = 1.0 / math.sqrt(2.0 * math.pi)
    token_count = pre_act.shape[1]
    token_scale = 1.0 / math.sqrt(token_count)
    module_ids = jnp.arange(sharer_counts.shape[0], dtype=jnp.int32)
    lookup = (path_table[:, None] == module_ids[None, :]).astype(jnp.float32)
    divisor = jnp.sum(lookup * sharer_counts[None, :].astype(jnp.float32), axis=1)
    sharing = (path_table[:, None] == path_table[None, :]).astype(jnp.float32) / divisor[:, None]
    inputs = pre_act[0].astype(jnp.float32)
    normal_cdf = 0.5 * (1.0 + jax.scipy.special.erf(inputs * inv_root_two))
    hidden = (inputs * normal_cdf).astype(jnp.bfloat16)
    gradient_slope = normal_cdf + inputs * jnp.exp(-0.5 * inputs * inputs) * inv_root_tau
    weights = w_down[0]
    block_rows = lax.all_gather(cotangent[0], "tp", axis=0, tiled=True)
    grad_sum = lax.dot_general(
        hidden, block_rows, (((0,), (0,)), ((), ())), preferred_element_type=jnp.float32
    )
    back_rows = lax.dot_general(
        block_rows, weights, (((1,), (1,)), ((), ())), preferred_element_type=jnp.float32
    )
    delta_rows = back_rows * gradient_slope
    grad_sum, delta_rows = (grad_sum, delta_rows)
    gradient = grad_sum * token_scale
    pre_grad = delta_rows.astype(jnp.bfloat16)[None]
    moment_one = 0.9 * first_moment[0] + 0.1 * gradient
    moment_two = 0.95 * second_moment[0] + 0.05 * gradient * gradient
    blended = blend_rows(
        sharing,
        (
            lax.all_to_all(gradient[None], "grp", split_axis=2, concat_axis=0, tiled=True),
            lax.all_to_all(moment_one[None], "grp", split_axis=2, concat_axis=0, tiled=True),
            lax.all_to_all(moment_two[None], "grp", split_axis=2, concat_axis=0, tiled=True),
        ),
    )
    grad_mean = lax.all_to_all(blended[0], "grp", split_axis=0, concat_axis=2, tiled=True)
    first_avg = lax.all_to_all(blended[1], "grp", split_axis=0, concat_axis=2, tiled=True)
    second_avg = lax.all_to_all(blended[2], "grp", split_axis=0, concat_axis=2, tiled=True)
    return (grad_mean.astype(jnp.bfloat16), first_avg, second_avg, pre_grad)


def solution(mesh):
    placed = (
        P("grp", None, "tp"),
        P("grp", "tp", None),
        P("grp", "tp", None),
        P("grp", "tp", None),
        P("grp", "tp", None),
        P(),
        P(),
    )
    return jax.shard_map(
        per_device,
        mesh=mesh,
        in_specs=placed,
        out_specs=(
            P("grp", "tp", None),
            P("grp", "tp", None),
            P("grp", "tp", None),
            P("grp", None, "tp"),
        ),
        check_vma=False,
    )
```

profile of v0, /device:TPU:6, one launch (start us, length us, event | category | flops | bytes accessed | tf_op | source)
XLA Modules:
  0.0 453.2 jit_solution(11108226900361579944)
XLA Ops:
  7.9 112.1 %all-gather.3.cloned.1.call-done = bf16[1,2048,2048]{2,1,0:T(8,128)(2,1)} async-done(((bf16[1,128,2048]{2,1,0:T(8,128)(2,1)}), bf16[1,2048,2048]{2,1,0:T(8,128)(2,1)}) %all-gather.3.cloned.1.call-update) | async-done | bytes 8388624 | tf_op jit(solution)/shard_map/all_gather | solution.py:32
  120.0 9.8 %fusion.26 = (f32[1,256,2048]{2,1,0:T(8,128)}, f32[1,256,2048]{2,1,0:T(8,128)S(1)}, f32[1,256,2048]{2,1,0:T(8,128)}) fusion(f32[1,256,2048]{2,1,0:T(8,128)} %param.11, f32[1,256,2048]{2,1,0:T(8,128)} %param.10, bf16[1,2048,2048]{2,1,0:T(8,128)(2,1)} %all-gather.3.cloned.1.call-done, bf16[1,2048,256]{2,1,0:T(8,128)(2,1)} %param.7), kind=kOutput, calls=%fused_computation.26 | convolution fusion | flops 2154823680 | bytes 19922944 | tf_op jit(solution)/shard_map/dot_general | solution.py:33
  129.8 6.0 %copy.28 = f32[1,256,2048]{1,0,2:T(1,128)} copy(f32[1,256,2048]{2,1,0:T(8,128)} %get-tuple-element.8) | data formatting | bytes 4194304 | tf_op jit(solution)/shard_map/broadcast_in_dim | solution.py:50
  135.9 4.5 all-to-all-start.4
  140.3 6.0 %copy.20 = f32[1,256,2048]{1,0,2:T(1,128)} copy(f32[1,256,2048]{2,1,0:T(8,128)} %get-tuple-element.10) | data formatting | bytes 4194304 | tf_op jit(solution)/shard_map/broadcast_in_dim | solution.py:48
  146.4 46.7 %all-to-all-done.4 = f32[1,256,2048]{1,0,2:T(1,128)} async-done(((f32[1,256,2048]{1,0,2:T(1,128)}), f32[1,256,2048]{1,0,2:T(1,128)}, u32[]{:S(2)}, u32[]{:S(2)}) %all-to-all-start.4) | async-done | bytes 2097184 | tf_op jit(solution)/shard_map/all_to_all | solution.py:50
  193.1 4.4 all-to-all-start
  197.5 3.6 copy.24
  201.1 46.5 %all-to-all-done = f32[1,256,2048]{1,0,2:T(1,128)} async-done(((f32[1,256,2048]{1,0,2:T(1,128)}), f32[1,256,2048]{1,0,2:T(1,128)}, u32[]{:S(2)}, u32[]{:S(2)}) %all-to-all-start) | async-done | bytes 2097184 | tf_op jit(solution)/shard_map/all_to_all | solution.py:48
  247.7 3.7 all-to-all-start.2
  251.6 3.0 copy.38
  254.7 3.0 copy.35
  257.7 3.5 fusion.24
  262.4 39.4 %all-to-all-done.2 = f32[1,256,2048]{1,0,2:T(1,128)S(1)} async-done(((f32[1,256,2048]{1,0,2:T(1,128)}), f32[1,256,2048]{1,0,2:T(1,128)S(1)}, u32[]{:S(2)}, u32[]{:S(2)}) %all-to-all-start.2) | async-done | bytes 2097184 | tf_op jit(solution)/shard_map/all_to_all | solution.py:49
  301.8 4.3 all-to-all-start.1
  306.2 3.0 copy.40
  315.4 18.1 %all-to-all-done.1 = bf16[16,256,128]{2,1,0:T(8,128)(2,1)} async-done(((bf16[16,256,128]{2,1,0:T(8,128)(2,1)}), bf16[16,256,128]{2,1,0:T(8,128)(2,1)}, u32[]{:S(2)}, u32[]{:S(2)}) %all-to-all-start.1) | async-done | bytes 1048608 | tf_op jit(solution)/shard_map/all_to_all | solution.py:53
  333.5 4.6 %all-to-all-start.5 = ((f32[16,256,128]{2,1,0:T(8,128)}), f32[16,256,128]{2,1,0:T(8,128)}, u32[]{:S(2)}, u32[]{:S(2)}) async-start(f32[16,256,128]{2,1,0:T(8,128)} %copy.30), calls=%async_computation.5 | async-start | bytes 4194304 | tf_op jit(solution)/shard_map/all_to_all | solution.py:55
  345.7 41.7 %all-to-all-done.5 = f32[16,256,128]{2,1,0:T(8,128)} async-done(((f32[16,256,128]{2,1,0:T(8,128)}), f32[16,256,128]{2,1,0:T(8,128)}, u32[]{:S(2)}, u32[]{:S(2)}) %all-to-all-start.5) | async-done | bytes 2097184 | tf_op jit(solution)/shard_map/all_to_all | solution.py:55
  387.5 3.7 all-to-all-start.3
  391.2 7.6 %fusion.10 = bf16[1,2048,256]{2,1,0:T(8,128)(2,1)} fusion(bf16[1,2048,2048]{2,1,0:T(8,128)(2,1)} %all-gather.3.cloned.1.call-done, bf16[1,256,2048]{2,1,0:T(8,128)(2,1)S(1)} %copy-done, bf16[1,2048,256]{2,1,0:T(8,128)(2,1)} %param.7), kind=kOutput, calls=%fused_computation.11 | convolution fusion | flops 2153250816 | bytes 11534336 | tf_op jit(solution)/shard_map/dot_general | solution.py:36
  403.4 2.9 copy.31
  406.3 2.9 copy.34
  409.1 32.5 %all-to-all-done.3 = f32[16,256,128]{2,1,0:T(8,128)S(1)} async-done(((f32[16,256,128]{2,1,0:T(8,128)}), f32[16,256,128]{2,1,0:T(8,128)S(1)}, u32[]{:S(2)}, u32[]{:S(2)}) %all-to-all-start.3) | async-done | bytes 2097184 | tf_op jit(solution)/shard_map/all_to_all | solution.py:54
  (26 shorter events, 25.2 us)
Async XLA Ops:
  7.2 384.0 %copy-start = (bf16[1,256,2048]{2,1,0:T(8,128)(2,1)S(1)}, bf16[1,256,2048]{2,1,0:T(8,128)(2,1)}, u32[]{:S(2)}) copy-start(bf16[1,256,2048]{2,1,0:T(8,128)(2,1)} %param.9) | copy-start | bytes 3145732
  7.2 112.9 %all-gather.3.cloned.1.call-start = ((), (), s32[]{:S(2)}) async-start(), calls=%async_computation.6 | async-start | bytes 8912896 | tf_op jit(solution)/shard_map/all_gather | solution.py:32
  135.9 57.2 %all-to-all-start.4 = ((f32[1,256,2048]{1,0,2:T(1,128)}), f32[1,256,2048]{1,0,2:T(1,128)}, u32[]{:S(2)}, u32[]{:S(2)}) async-start(f32[1,256,2048]{1,0,2:T(1,128)} %copy.28), calls=%async_computation.4 | async-start | bytes 4194304 | tf_op jit(solution)/shard_map/all_to_all | solution.py:50
  193.1 54.6 %all-to-all-start = ((f32[1,256,2048]{1,0,2:T(1,128)}), f32[1,256,2048]{1,0,2:T(1,128)}, u32[]{:S(2)}, u32[]{:S(2)}) async-start(f32[1,256,2048]{1,0,2:T(1,128)} %copy.20), calls=%async_computation | async-start | bytes 4194304 | tf_op jit(solution)/shard_map/all_to_all | solution.py:48
  201.1 50.2 %copy-start.4 = (s32[16]{0:T(128)S(1)}, s32[16]{0:T(128)}, u32[]{:S(2)}) copy-start(s32[16]{0:T(128)} %param.13) | copy-start | bytes 196
  201.1 50.3 %copy-start.3 = (s32[16]{0:T(128)S(1)}, s32[16]{0:T(128)}, u32[]{:S(2)}) copy-start(s32[16]{0:T(128)} %param.12) | copy-start | bytes 196
  247.7 54.1 %all-to-all-start.2 = ((f32[1,256,2048]{1,0,2:T(1,128)}), f32[1,256,2048]{1,0,2:T(1,128)S(1)}, u32[]{:S(2)}, u32[]{:S(2)}) async-start(f32[1,256,2048]{1,0,2:T(1,128)} %copy.24), calls=%async_computation.2 | async-start | bytes 4194304 | tf_op jit(solution)/shard_map/all_to_all | solution.py:49
  301.8 7.4 %copy-start.1 = (f32[1,256,2048]{1,0,2:T(1,128)}, f32[1,256,2048]{1,0,2:T(1,128)S(1)}, u32[]{:S(2)}) copy-start(f32[1,256,2048]{1,0,2:T(1,128)S(1)} %all-to-all-done.2) | copy-start | bytes 6291460
  301.8 31.7 %all-to-all-start.1 = ((bf16[16,256,128]{2,1,0:T(8,128)(2,1)}), bf16[16,256,128]{2,1,0:T(8,128)(2,1)}, u32[]{:S(2)}, u32[]{:S(2)}) async-start(bf16[16,256,128]{2,1,0:T(8,128)(2,1)} %copy.22), calls=%async_computation.1 | async-start | bytes 2097152 | tf_op jit(solution)/shard_map/all_to_all | solution.py:53
  315.4 22.8 %copy-start.2 = (f32[1,256,2048]{1,0,2:T(1,128)S(1)}, f32[1,256,2048]{1,0,2:T(1,128)}, u32[]{:S(2)}) copy-start(f32[1,256,2048]{1,0,2:T(1,128)} %copy-done.1) | copy-start | bytes 6291460
  333.5 54.0 %all-to-all-start.5 = ((f32[16,256,128]{2,1,0:T(8,128)}), f32[16,256,128]{2,1,0:T(8,128)}, u32[]{:S(2)}, u32[]{:S(2)}) async-start(f32[16,256,128]{2,1,0:T(8,128)} %copy.30), calls=%async_computation.5 | async-start | bytes 4194304 | tf_op jit(solution)/shard_map/all_to_all | solution.py:55
  387.5 54.2 %all-to-all-start.3 = ((f32[16,256,128]{2,1,0:T(8,128)}), f32[16,256,128]{2,1,0:T(8,128)S(1)}, u32[]{:S(2)}, u32[]{:S(2)}) async-start(f32[16,256,128]{2,1,0:T(8,128)} %copy.26), calls=%async_computation.3 | async-start | bytes 4194304 | tf_op jit(solution)/shard_map/all_to_all | solution.py:54
Sparse Core Ops, SparseCore 0:
  10.7 109.2 all-gather.2
where the time goes:
time: 456 us; the launch traced here: 453 us
  waiting for transfers between devices  338 us (74%)
  local copies, waits for them, and re-layouts  51 us (11%)
  starting transfers between devices  25.4 us (6%)
  matrix products  24.8 us (5%)
  between operations  14.2 us (3%)
    all_gather x1, waiting for transfers between devices, per_device(): block_rows = lax.all_gather(cotangent[0], 'tp', axis=0, tiled=True)  112 us
    all_to_all x1, waiting for transfers between devices, per_device(): lax.all_to_all(moment_two[None], 'grp', split_axis=2, concat_axis=0, tile...  46.7 us
    all_to_all x1, waiting for transfers between devices, per_device(): lax.all_to_all(gradient[None], 'grp', split_axis=2, concat_axis=0, tiled=...  46.5 us
    all_to_all x1, waiting for transfers between devices, per_device(): lax.all_to_all(blended[2], 'grp', split_axis=0, concat_axis=2, tiled=True)  41.7 us
    all_to_all x1, waiting for transfers between devices, per_device(): lax.all_to_all(moment_one[None], 'grp', split_axis=2, concat_axis=0, tile...  39.4 us
    all_to_all x1, waiting for transfers between devices, per_device(): lax.all_to_all(blended[1], 'grp', split_axis=0, concat_axis=2, tiled=True)  32.5 us
    all_to_all x1, waiting for transfers between devices, per_device(): lax.all_to_all(blended[0], 'grp', split_axis=0, concat_axis=2, tiled=True)  18.1 us
    unnamed x16, local copies, waits for them, and re-layouts  15.6 us
  transfers between devices with their start and end apart: 7, of which 7 were waited for; matrix products, arithmetic and copies ran while one was open for 12% of the time, Pallas kernels for 0%

commit v1 on v0

v1 whole, which is shorter than its diff:
```python
import functools
import math

import jax
import jax.numpy as jnp
from jax import lax
from jax.experimental import pallas as pl
from jax.experimental.pallas import tpu as pltpu
from jax.sharding import PartitionSpec as P

MESH = pl.DeviceIdType.MESH
COLS = 256
NY = 4
NZ = 4
NX = 4
SLOTS = 4
LAG_END, LAG_MID, LAG_AVG, LAG_RET, LAG_OUT = 2, 4, 6, 8, 10

INV_ROOT_TWO = 1.0 / math.sqrt(2.0)
INV_ROOT_TAU = 1.0 / math.sqrt(2.0 * math.pi)


def kernel(
    chunks, block, quarter, scale,
    table, pre_act, cot, w_down, first, second,
    grad_out, first_out, second_out, pre_out,
    gbuf, hid_t, slope, grad, mine, raw, slots, from_end, from_mid, avg, back, ret,
    cot_send, group_send, z_sem, x_sem, c_sem, raw_sem, end_sem, mid_sem, ret_sem,
):
    f32, bf16 = jnp.float32, jnp.bfloat16
    units = 3 * chunks
    g, t = lax.axis_index("grp"), lax.axis_index("tp")
    y, zl = g // NZ, lax.rem(g, NZ)
    zh, x, core = t // (2 * NX), lax.rem(t // 2, NX), lax.rem(t, 2)
    is_mid = jnp.logical_or(zl == 1, zl == 2)
    mate = jnp.where(is_mid, jnp.where(zl == 1, 0, 3), jnp.where(zl == 0, 1, 2))
    mate_id = (y * NZ + mate, t)
    mid_id = (y * NZ + 3 - zl, t)
    y_ids = [(lax.rem(y + d, NY) * NZ + zl, t) for d in (1, 2, 3)]
    x_ids = [(g, zh * 2 * NX + lax.rem(x + d, NX) * 2 + core) for d in (1, 3, 2)]
    z_id = (g, (1 - zh) * 2 * NX + x * 2 + core)
    c_id = (g, zh * 2 * NX + x * 2 + 1 - core)

    pair_at = pl.multiple_of((core * NX + x) * 2 * block, 2 * block)
    own_at = pl.multiple_of(pair_at + zh * block, block)
    half_at = pl.multiple_of(core * NX * 2 * block, NX * 2 * block)

    barrier = pltpu.get_barrier_semaphore()
    for peer in [z_id, c_id, mate_id] + x_ids + y_ids:
        pl.semaphore_signal(barrier, inc=1, device_id=peer, device_id_type=MESH)

    @pl.when(is_mid)
    def _():
        pl.semaphore_signal(barrier, inc=1, device_id=mid_id, device_id_type=MESH)

    for c in range(chunks):
        gbuf[c, pl.ds(own_at, block), :] = cot[:, c * COLS:(c + 1) * COLS]

    pl.semaphore_wait(barrier, jnp.where(is_mid, 10, 9))

    def send(src, dst, ssem, rsem, peer):
        pltpu.make_async_remote_copy(
            src_ref=src, dst_ref=dst, send_sem=ssem, recv_sem=rsem,
            device_id=peer, device_id_type=MESH,
        ).start()

    def wait(ref, sem):
        pltpu.make_async_copy(ref, ref, sem).wait()

    def columns(c):
        return pl.ds(pl.multiple_of(c * COLS, COLS), COLS)

    def quarter_rows(owner):
        return pl.ds(pl.multiple_of(owner * quarter, quarter), quarter)

    def send_raw(u):
        for d in range(3):
            owner = lax.rem(y + d + 1, NY)
            send(mine.at[u, quarter_rows(owner)], raw.at[u, d], group_send.at[0], raw_sem.at[u], y_ids[d])

    def column_slots(u, r):
        parts = [mine[u, pl.ds(pl.multiple_of(y * quarter + r * 16, 16), 16), :].astype(f32)]
        parts += [raw[u, d, pl.ds(r * 16, 16), :].astype(f32) for d in range(3)]
        group = [lax.rem(y - d + NY, NY) * NZ + zl for d in range(4)]
        out = []
        for s in range(SLOTS):
            total = table[s * 16 + group[0]] * parts[0]
            for d in range(1, 4):
                total += table[s * 16 + group[d]] * parts[d]
            out.append(total)
        return out

    def send_back(u, held, scaled):
        for r in range(quarter // 16):
            rows = pl.ds(r * 16, 16)
            parts = [held[u, s, rows, :].astype(f32) for s in range(SLOTS)]
            for d in range(4):
                group = lax.rem(y + d, NY) * NZ + zl
                total = table[group] * parts[0]
                for s in range(1, SLOTS):
                    total += table[s * 16 + group] * parts[s]
                if d == 0:
                    ret[u, pl.ds(pl.multiple_of(y * quarter + r * 16, 16), 16), :] = total.astype(bf16)
                else:
                    back[u, d - 1, rows, :] = total.astype(bf16)
        for d in range(3):
            send(back.at[u, d], ret.at[u, quarter_rows(y)], group_send.at[2], ret_sem.at[u], y_ids[d])

    def tick(i, carry):
        @pl.when(jnp.logical_and(lax.rem(i, 2) == 0, i < 2 * chunks))
        def _():
            c = i // 2
            part = gbuf.at[c, pl.ds(own_at, block)]
            send(part, part, cot_send.at[0], z_sem.at[c], z_id)

        @pl.when(jnp.logical_and(lax.rem(i, 2) == 1, i < 2 * chunks + 1))
        def _():
            c = i // 2
            wait(gbuf.at[c, pl.ds(own_at, block)], z_sem.at[c])
            part = gbuf.at[c, pl.ds(pair_at, 2 * block)]
            for k in range(3):
                send(part, part, cot_send.at[1], x_sem.at[c], x_ids[k])

        @pl.when(jnp.logical_and(lax.rem(i, 2) == 0, jnp.logical_and(i >= 4, i < 2 * chunks + 4)))
        def _():
            c = i // 2 - 2
            wait(gbuf.at[c, pl.ds(0, 6 * block)], x_sem.at[c])
            part = gbuf.at[c, pl.ds(half_at, NX * 2 * block)]
            send(part, part, cot_send.at[2], c_sem.at[c], c_id)

        @pl.when(i < chunks)
        def _():
            mine[i] = first[:, columns(i)].astype(bf16)
            send_raw(i)
            place_core, place_x = i // NX, lax.rem(i, NX)
            for half in range(2):
                rows = pl.ds(pl.multiple_of((half * 2 * NX + place_x * 2 + place_core) * block, block), block)
                put = pl.ds(pl.multiple_of((i * 2 + half) * block, block), block)
                inputs = pre_act[rows, :].astype(f32)
                cdf = 0.5 * (1.0 + lax.erf(inputs * INV_ROOT_TWO))
                slope[put, :] = cdf + inputs * jnp.exp(-0.5 * inputs * inputs) * INV_ROOT_TAU
                hid_t[:, put] = (inputs * cdf).T.astype(bf16)

        @pl.when(jnp.logical_and(i >= chunks, jnp.logical_and(i < units, lax.rem(i - chunks, 2) == 0)))
        def _():
            c = (i - chunks) // 2
            wait(gbuf.at[c, pl.ds(0, NX * 2 * block)], c_sem.at[c])
            value = jnp.dot(hid_t[...], gbuf[c], preferred_element_type=f32) * scale
            grad[c] = value
            mine[i] = value.astype(bf16)
            send_raw(i)

        @pl.when(jnp.logical_and(i >= chunks, jnp.logical_and(i < units, lax.rem(i - chunks, 2) == 1)))
        def _():
            c = (i - chunks) // 2
            value = grad[c]
            mine[i] = (0.95 * second[:, columns(c)] + 0.05 * value * value).astype(bf16)
            send_raw(i)

        u = i - LAG_END

        @pl.when(jnp.logical_and(jnp.logical_not(is_mid), jnp.logical_and(u >= 0, u < units)))
        def _():
            wait(raw.at[u], raw_sem.at[u])
            for r in range(quarter // 16):
                sums = column_slots(u, r)
                for s in range(SLOTS):
                    slots[u, s, pl.ds(r * 16, 16), :] = sums[s].astype(bf16)
            send(slots.at[u], from_end.at[u], group_send.at[1], end_sem.at[u], mate_id)

        m = i - LAG_MID

        @pl.when(jnp.logical_and(is_mid, jnp.logical_and(m >= 0, m < units)))
        def _():
            wait(raw.at[m], raw_sem.at[m])
            wait(from_end.at[m], end_sem.at[m])
            for r in range(quarter // 16):
                sums = column_slots(m, r)
                for s in range(SLOTS):
                    rows = pl.ds(r * 16, 16)
                    slots[m, s, rows, :] = (sums[s] + from_end[m, s, rows, :].astype(f32)).astype(bf16)
            send(slots.at[m], from_mid.at[m], group_send.at[1], mid_sem.at[m], mid_id)

        v = i - LAG_AVG

        @pl.when(jnp.logical_and(is_mid, jnp.logical_and(v >= 0, v < units)))
        def _():
            wait(from_mid.at[v], mid_sem.at[v])
            for r in range(quarter // 16):
                rows = pl.ds(r * 16, 16)
                for s in range(SLOTS):
                    total = slots[v, s, rows, :].astype(f32) + from_mid[v, s, rows, :].astype(f32)
                    avg[v, s, rows, :] = (table[64 + s] * total).astype(bf16)
            send(avg.at[v], from_end.at[v], group_send.at[3], end_sem.at[v], mate_id)
            send_back(v, avg, True)

        b = i - LAG_RET

        @pl.when(jnp.logical_and(jnp.logical_not(is_mid), jnp.logical_and(b >= 0, b < units)))
        def _():
            wait(from_end.at[b], end_sem.at[b])
            send_back(b, from_end, False)

        o = i - LAG_OUT
        alone = table[80 + g]

        @pl.when(jnp.logical_and(o >= 0, o < units))
        def _():
            wait(raw.at[o], ret_sem.at[o])

        @pl.when(jnp.logical_and(o >= chunks, jnp.logical_and(o < units, lax.rem(o - chunks, 2) == 0)))
        def _():
            c = (o - chunks) // 2
            cols = columns(c)
            for r in range(4):
                rows = pl.ds(r * quarter, quarter)
                own = grad[c, rows, :]
                mean = ret[o, rows, :].astype(f32)
                grad_out[rows, cols] = (mean + alone * own).astype(bf16)
                first_out[rows, cols] = (
                    0.9 * ret[c, rows, :].astype(f32) + 0.1 * mean
                    + alone * (0.9 * first[rows, cols] + 0.1 * own)
                )

        @pl.when(jnp.logical_and(o >= chunks, jnp.logical_and(o < units, lax.rem(o - chunks, 2) == 1)))
        def _():
            c = (o - chunks) // 2
            cols = columns(c)
            for r in range(4):
                rows = pl.ds(r * quarter, quarter)
                own = grad[c, rows, :]
                second_out[rows, cols] = ret[o, rows, :].astype(f32) + alone * (
                    0.95 * second[rows, cols] + 0.05 * own * own
                )

        p = i - (units - 1)

        @pl.when(jnp.logical_and(p >= 0, p < 2 * NX))
        def _():
            here = pl.ds(pl.multiple_of(p * 2 * block, 2 * block), 2 * block)
            total = jnp.zeros((2 * block, pre_act.shape[1]), f32)
            for c in range(chunks):
                total += lax.dot_general(
                    gbuf[c, here, :], w_down[:, c * COLS:(c + 1) * COLS],
                    (((1,), (1,)), ((), ())), preferred_element_type=f32,
                )
            total = (total * slope[here, :]).astype(bf16)
            place_core, place_x = p // NX, lax.rem(p, NX)
            for half in range(2):
                rows = pl.ds(pl.multiple_of((half * 2 * NX + place_x * 2 + place_core) * block, block), block)
                pre_out[rows, :] = total[half * block:(half + 1) * block]

        return carry

    lax.fori_loop(0, units + LAG_OUT, tick, 0)

    wait(gbuf.at[:, pl.ds(0, block)], cot_send.at[0])
    wait(gbuf.at[:, pl.ds(0, 6 * block)], cot_send.at[1])
    wait(gbuf.at[:, pl.ds(0, 2 * NX * block)], cot_send.at[2])
    wait(raw, group_send.at[0])
    wait(slots, group_send.at[1])
    wait(raw, group_send.at[2])

    @pl.when(is_mid)
    def _():
        wait(avg, group_send.at[3])


def sharing_table(path_table, sharer_counts):
    f32 = jnp.float32
    ids = jnp.arange(path_table.shape[0], dtype=jnp.int32)
    same = path_table[:, None] == path_table[None, :]
    leader = jnp.min(jnp.where(same, ids[None, :], ids.shape[0]), axis=1)
    shared = jnp.sum(same.astype(jnp.int32), axis=1) > 1
    opens = jnp.logical_and(shared, leader == ids)
    slot = jnp.sum(jnp.logical_and(opens[None, :], ids[None, :] < leader[:, None]).astype(jnp.int32), axis=1)
    member = jnp.logical_and(shared[None, :], slot[None, :] == jnp.arange(SLOTS, dtype=jnp.int32)[:, None])
    modules = jnp.arange(sharer_counts.shape[0], dtype=jnp.int32)
    lookup = path_table[:, None] == modules[None, :]
    count = jnp.sum(jnp.where(lookup, sharer_counts[None, :], 0), axis=1).astype(f32)
    inverse = jnp.max(jnp.where(member, 1.0 / count[None, :], 0.0), axis=1)
    alone = jnp.where(shared, 0.0, 1.0 / count)
    rows = [member.astype(f32).reshape(-1), jnp.pad(inverse, (0, 16 - SLOTS)), alone]
    return jnp.concatenate(rows)


def per_device(pre_act, cotangent, w_down, first_moment, second_moment, path_table, sharer_counts):
    f32, bf16 = jnp.float32, jnp.bfloat16
    block, width = cotangent.shape[1:]
    tokens, hidden = pre_act.shape[1:]
    chunks, quarter = width // COLS, hidden // NY
    units = 3 * chunks
    table = sharing_table(path_table, sharer_counts)
    vmem = pl.BlockSpec(memory_space=pltpu.VMEM)
    held = pltpu.VMEM((units, SLOTS, quarter, COLS), bf16)
    ring = pltpu.VMEM((units, 3, quarter, COLS), bf16)
    whole = pltpu.VMEM((units, hidden, COLS), bf16)
    outs = pl.pallas_call(
        functools.partial(kernel, chunks, block, quarter, 1.0 / math.sqrt(tokens)),
        out_shape=(
            jax.ShapeDtypeStruct((hidden, width), bf16),
            jax.ShapeDtypeStruct((hidden, width), f32),
            jax.ShapeDtypeStruct((hidden, width), f32),
            jax.ShapeDtypeStruct((tokens, hidden), bf16),
        ),
        in_specs=[pl.BlockSpec(memory_space=pltpu.SMEM)] + [vmem] * 5,
        out_specs=(vmem,) * 4,
        scratch_shapes=[
            pltpu.VMEM((chunks, tokens, COLS), bf16),
            pltpu.VMEM((hidden, tokens), bf16),
            pltpu.VMEM((tokens, hidden), f32),
            pltpu.VMEM((chunks, hidden, COLS), f32),
            whole,
            ring,
            held,
            held,
            held,
            held,
            ring,
            whole,
            pltpu.SemaphoreType.DMA((3,)),
            pltpu.SemaphoreType.DMA((4,)),
            pltpu.SemaphoreType.DMA((chunks,)),
            pltpu.SemaphoreType.DMA((chunks,)),
            pltpu.SemaphoreType.DMA((chunks,)),
            pltpu.SemaphoreType.DMA((units,)),
            pltpu.SemaphoreType.DMA((units,)),
            pltpu.SemaphoreType.DMA((units,)),
            pltpu.SemaphoreType.DMA((units,)),
        ],
        compiler_params=pltpu.CompilerParams(
            collective_id=0, has_side_effects=True, vmem_limit_bytes=60 * 2**20
        ),
        cost_estimate=pl.CostEstimate(
            flops=4 * tokens * hidden * width, bytes_accessed=13 * 2**20, transcendentals=2 * tokens * hidden
        ),
        name="routed_down_grad",
    )(table, pre_act[0], cotangent[0], w_down[0], first_moment[0], second_moment[0])
    return tuple(out[None] for out in outs)


def solution(mesh):
    placed = (
        P("grp", None, "tp"),
        P("grp", "tp", None),
        P("grp", "tp", None),
        P("grp", "tp", None),
        P("grp", "tp", None),
        P(),
        P(),
    )
    return jax.shard_map(
        per_device,
        mesh=mesh,
        in_specs=placed,
        out_specs=(
            P("grp", "tp", None),
            P("grp", "tp", None),
            P("grp", "tp", None),
            P("grp", None, "tp"),
        ),
        check_vma=False,
    )
```

time: 456 us -> 135 us (0.30)
  waiting for transfers between devices: 338 us -> 0 us
  Pallas kernels: 0 us -> 125 us
  local copies, waits for them, and re-layouts: 51 us -> 7.81 us
  starting transfers between devices: 25.4 us -> 0 us
  matrix products: 24.8 us -> 0 us
  between operations: 14.2 us -> 0.67 us
    all_to_all x6 -> x0, waiting for transfers between devices: 225 us -> none  [the longest x1 46.7 us: per_device(): lax.all_to_all(moment_two[None], 'grp', split_axis=2, concat_axis=0, tile...]
    pallas_call x0 -> x1, Pallas kernels: none -> 125 us  [per_device(): pl.pallas_call(functools.partial(kernel, chunks, block, quarter, 1.0 / ma...]
    all_gather x1 -> x0, waiting for transfers between devices: 112 us -> none  [per_device(): block_rows = lax.all_gather(cotangent[0], 'tp', axis=0, tiled=True)]
    all_to_all x6 -> x0, starting transfers between devices: 25.3 us -> none  [the longest x1 4.62 us: per_device(): lax.all_to_all(blended[2], 'grp', split_axis=0, concat_axis=2, tiled=True)]
    dot_general x5 -> x0, matrix products: 24.8 us -> none  [the longest x1 9.78 us: per_device(): lax.dot_general(hidden, block_rows, (((0,), (0,)), ((), ())), preferred_e...]
    broadcast_in_dim x3 -> x0, local copies, waits for them, and re-layouts: 15.7 us -> none  [the longest x1 6.03 us: per_device(): moment_two[None]]
    all_to_all x6 -> x0, local copies, waits for them, and re-layouts: 14.5 us -> none  [the longest x1 3.03 us: per_device(): lax.all_to_all(gradient[None], 'grp', split_axis=2, concat_axis=0, tiled=...]
    unnamed x16 -> x10, local copies, waits for them, and re-layouts: 15.6 us -> 7.73 us
  transfers between devices with their start and end apart: 7 -> 0, of which waited for: 7 -> 0; matrix products, arithmetic and copies ran while one was open for 12% -> 0% of each run, Pallas kernels for 0% -> 0%
where the time goes in v1:
time: 135 us
  Pallas kernels  125 us (93%)
  local copies, waits for them, and re-layouts  7.81 us (6%)
  other arithmetic  1.87 us (1%)
    pallas_call x1, Pallas kernels, per_device(): pl.pallas_call(functools.partial(kernel, chunks, block, quarter, 1.0 / ma...  125 us
    unnamed x10, local copies, waits for them, and re-layouts  7.73 us

profile of v1, /device:TPU:6, one launch (start us, length us, event | category | flops | bytes accessed | tf_op | source)
XLA Modules:
  0.0 135.1 jit_solution(1631778433375719767)
XLA Ops:
  0.6 0.9 fusion
  1.6 0.2 convert_reduce_fusion
  1.8 0.1 select_reduce_fusion.1
  1.9 0.1 reshape.38
  2.0 0.6 fusion.6.table
  2.6 124.7 %routed_down_grad.1 = (bf16[256,2048]{1,0:T(8,128)(2,1)}, f32[256,2048]{1,0:T(8,128)}, f32[256,2048]{1,0:T(8,128)}, bf16[2048,256]{1,0:T(8,128)(2,1)}) custom-call(f32[96]{0:T(128)} %fusion.6.table, bf16[2048,256]{1,0:T(8,128)(2,1)} %bitcast.15, bf16[128,2048]{1,0:T(8,128)(2,1)} %bitcast.17, bf16[256,2048]{1,0:T(8,128)(2,1)} %bitcast.16, ...), custom_call_target="tpu_custom_call" | custom-call | flops 4294967296 | bytes 13631488 | tf_op jit(solution)/shard_map/routed_down_grad/pallas_call | solution.py:298
  127.4 0.0 copy-start.1
  127.4 2.5 %copy.15 = bf16[1,256,2048]{2,1,0:T(8,128)(2,1)} copy(bf16[1,256,2048]{2,1,0:T(8,128)(2,1)} %bitcast.12) | data formatting | bytes 2097152
  129.8 0.0 copy-done.1
  129.8 0.0 copy-start
  129.8 1.3 copy.16
  131.1 1.0 copy-done
  132.2 0.0 copy-start.2
  132.2 1.3 copy.17
  133.5 0.6 copy-done.2
  134.1 1.0 copy.18
  (3 shorter events, 0.0 us)
Async XLA Ops:
  127.4 2.5 %copy-start.1 = (f32[256,2048]{1,0:T(8,128)S(1)}, f32[256,2048]{1,0:T(8,128)}, u32[]{:S(2)}) copy-start(f32[256,2048]{1,0:T(8,128)} %get-tuple-element.9) | copy-start | bytes 6291460
  129.8 2.3 %copy-start = (f32[256,2048]{1,0:T(8,128)S(1)}, f32[256,2048]{1,0:T(8,128)}, u32[]{:S(2)}) copy-start(f32[256,2048]{1,0:T(8,128)} %get-tuple-element.10) | copy-start | bytes 6291460
  132.2 2.0 %copy-start.2 = (bf16[2048,256]{1,0:T(8,128)(2,1)S(1)}, bf16[2048,256]{1,0:T(8,128)(2,1)}, u32[]{:S(2)}) copy-start(bf16[2048,256]{1,0:T(8,128)(2,1)} %get-tuple-element.11) | copy-start | bytes 3145732

commit v2 on v1

v2 whole, which is shorter than its diff:
```python
import functools
import math

import jax
import jax.numpy as jnp
from jax import lax
from jax.experimental import pallas as pl
from jax.experimental.pallas import tpu as pltpu
from jax.sharding import PartitionSpec as P

MESH = pl.DeviceIdType.MESH
COLS = 256
NY = 4
NZ = 4
NX = 4
FEWEST_SLOTS, MOST_SLOTS = 2, 4
LAG_END, LAG_MID, LAG_AVG, LAG_RET = 3, 6, 9, 12

B_AT, C_AT = 2, 7
AHEAD = 2
STEPS = 4

INV_ROOT_TWO = 1.0 / math.sqrt(2.0)
INV_ROOT_TAU = 1.0 / math.sqrt(2.0 * math.pi)


def kernel(
    nslots, chunks, block, quarter, scale,
    path, counts, pre_act_in, cot_in, w_down_in, first_in, second_in,
    ret, pre_out,
    table, pre_act, cot, w_down, first, second,
    gbuf, hid_t, slope, grad, mine, raw, slots, from_end, from_mid, avg, back, pre,
    load_sem, store_sem, cot_send, group_send, z_sem, x_sem, c_sem, raw_sem, end_sem, mid_sem, ret_sem,
):
    f32, bf16 = jnp.float32, jnp.bfloat16
    units = 3 * chunks
    g, t = lax.axis_index("grp"), lax.axis_index("tp")
    y, zl = g // NZ, lax.rem(g, NZ)
    zh, x, core = t // (2 * NX), lax.rem(t // 2, NX), lax.rem(t, 2)
    is_mid = jnp.logical_or(zl == 1, zl == 2)
    mate = jnp.where(is_mid, jnp.where(zl == 1, 0, 3), jnp.where(zl == 0, 1, 2))
    mate_id = (y * NZ + mate, t)
    mid_id = (y * NZ + 3 - zl, t)
    y_ids = [(lax.rem(y + d, NY) * NZ + zl, t) for d in (1, 2, 3)]
    x_ids = [(g, zh * 2 * NX + lax.rem(x + d, NX) * 2 + core) for d in (1, 3, 2)]
    z_id = (g, (1 - zh) * 2 * NX + x * 2 + core)
    c_id = (g, zh * 2 * NX + x * 2 + 1 - core)

    pair_at = pl.multiple_of((core * NX + x) * 2 * block, 2 * block)
    own_at = pl.multiple_of(pair_at + zh * block, block)
    other_at = pl.multiple_of(pair_at + (1 - zh) * block, block)
    half_at = pl.multiple_of(core * NX * 2 * block, NX * 2 * block)

    barrier = pltpu.get_barrier_semaphore()
    for peer in [z_id, c_id, mate_id] + x_ids + y_ids:
        pl.semaphore_signal(barrier, inc=1, device_id=peer, device_id_type=MESH)

    @pl.when(is_mid)
    def _():
        pl.semaphore_signal(barrier, inc=1, device_id=mid_id, device_id_type=MESH)

    loads = [(cot_in, cot), (first_in, first), (pre_act_in, pre_act), (second_in, second), (w_down_in, w_down)]
    loads = [pltpu.make_async_copy(src, dst, load_sem.at[k]) for k, (src, dst) in enumerate(loads)]
    for load in loads:
        load.start()
    fill_table(nslots, table, path, counts)
    loads[0].wait()
    for c in range(chunks):
        gbuf[c, pl.ds(own_at, block), :] = cot[:, c * COLS:(c + 1) * COLS]

    pl.semaphore_wait(barrier, jnp.where(is_mid, 10, 9))

    def send(src, dst, ssem, rsem, peer):
        pltpu.make_async_remote_copy(
            src_ref=src, dst_ref=dst, send_sem=ssem, recv_sem=rsem,
            device_id=peer, device_id_type=MESH,
        ).start()

    def wait(ref, sem):
        pltpu.make_async_copy(ref, ref, sem).wait()

    def columns(c):
        return pl.ds(pl.multiple_of(c * COLS, COLS), COLS)

    def quarter_rows(owner):
        return pl.ds(pl.multiple_of(owner * quarter, quarter), quarter)

    def send_x(c, at):
        part = gbuf.at[c, pl.ds(at, block)]
        for k in range(3):
            send(part, part, cot_send.at[1], x_sem.at[c], x_ids[k])

    def send_own(c):
        part = gbuf.at[c, pl.ds(own_at, block)]
        send(part, part, cot_send.at[0], z_sem.at[c], z_id)
        send_x(c, own_at)

    def send_raw(u):
        for d in range(3):
            owner = lax.rem(y + d + 1, NY)
            send(mine.at[u, quarter_rows(owner)], raw.at[u, d], group_send.at[0], raw_sem.at[u], y_ids[d])

    def column_parts(u, r):
        parts = [mine[u, pl.ds(pl.multiple_of(y * quarter + r * 16, 16), 16), :].astype(f32)]
        return parts + [raw[u, d, pl.ds(r * 16, 16), :].astype(f32) for d in range(3)]

    def column_slots(u, r):
        parts = column_parts(u, r)
        group = [lax.rem(y - d + NY, NY) * NZ + zl for d in range(4)]
        out = []
        for s in range(nslots):
            total = table[s * 16 + group[0]] * parts[0]
            for d in range(1, 4):
                total += table[s * 16 + group[d]] * parts[d]
            out.append(total)
        return out

    def send_back(u, held):
        for r in range(quarter // 16):
            rows = pl.ds(r * 16, 16)
            own = column_parts(u, r)
            parts = [held[u, s, rows, :].astype(f32) for s in range(nslots)]
            for d in range(4):
                group = lax.rem(y + d, NY) * NZ + zl
                total = table[group] * parts[0]
                for s in range(1, nslots):
                    total += table[s * 16 + group] * parts[s]
                for k in range(4):
                    total += table[80 + group * NY + lax.rem(y - k + NY, NY)] * own[k]
                back[u, d, rows, :] = total.astype(bf16)
        pltpu.make_async_copy(back.at[u, 0], ret.at[u, quarter_rows(y)], store_sem.at[0]).start()
        for d in range(3):
            send(back.at[u, d + 1], ret.at[u, quarter_rows(y)], group_send.at[2], ret_sem.at[0], y_ids[d])

    def tick(i, carry):
        @pl.when(i < chunks)
        def _():
            mine[i] = first[:, columns(i)].astype(bf16)
            send_raw(i)
            place_core, place_x = i // NX, lax.rem(i, NX)

            @pl.when(i == 0)
            def _():
                loads[2].wait()

            for half in range(2):
                rows = pl.ds(pl.multiple_of((half * 2 * NX + place_x * 2 + place_core) * block, block), block)
                put = pl.ds(pl.multiple_of((i * 2 + half) * block, block), block)
                inputs = pre_act[rows, :].astype(f32)
                cdf = 0.5 * (1.0 + lax.erf(inputs * INV_ROOT_TWO))
                slope[put, :] = cdf + inputs * jnp.exp(-0.5 * inputs * inputs) * INV_ROOT_TAU
                hid_t[:, put] = (inputs * cdf).T.astype(bf16)

        @pl.when(jnp.logical_and(i >= chunks, jnp.logical_and(i < units, lax.rem(i - chunks, 2) == 0)))
        def _():
            c = (i - chunks) // 2
            wait(gbuf.at[c, pl.ds(0, NX * 2 * block)], c_sem.at[c])
            value = jnp.dot(hid_t[...], gbuf[c], preferred_element_type=f32) * scale
            grad[...] = value
            mine[i] = value.astype(bf16)
            send_raw(i)

        @pl.when(jnp.logical_and(lax.rem(i, 2) == 0, jnp.logical_and(i >= B_AT, i < 2 * chunks + B_AT)))
        def _():
            c = (i - B_AT) // 2
            wait(gbuf.at[c, pl.ds(own_at, block)], z_sem.at[c])
            send_x(c, other_at)

            @pl.when(c < chunks - AHEAD)
            def _():
                send_own(c + AHEAD)

        @pl.when(jnp.logical_and(i >= chunks, jnp.logical_and(i < units, lax.rem(i - chunks, 2) == 1)))
        def _():
            c = (i - chunks) // 2

            @pl.when(c == 0)
            def _():
                loads[3].wait()

            value = grad[...]
            mine[i] = (0.95 * second[:, columns(c)] + 0.05 * value * value).astype(bf16)
            send_raw(i)

        @pl.when(jnp.logical_and(lax.rem(i, 2) == 1, jnp.logical_and(i >= C_AT, i < 2 * chunks + C_AT)))
        def _():
            c = (i - C_AT) // 2
            wait(gbuf.at[c, pl.ds(0, 6 * block)], x_sem.at[c])
            part = gbuf.at[c, pl.ds(half_at, NX * 2 * block)]
            send(part, part, cot_send.at[2], c_sem.at[c], c_id)

        u = i - LAG_END

        @pl.when(jnp.logical_and(jnp.logical_not(is_mid), jnp.logical_and(u >= 0, u < units)))
        def _():
            wait(raw.at[u], raw_sem.at[u])
            for r in range(quarter // 16):
                sums = column_slots(u, r)
                for s in range(nslots):
                    slots[u, s, pl.ds(r * 16, 16), :] = sums[s].astype(bf16)
            send(slots.at[u], from_end.at[u], group_send.at[1], end_sem.at[u], mate_id)

        m = i - LAG_MID

        @pl.when(jnp.logical_and(is_mid, jnp.logical_and(m >= 0, m < units)))
        def _():
            wait(raw.at[m], raw_sem.at[m])
            wait(from_end.at[m], end_sem.at[m])
            for r in range(quarter // 16):
                sums = column_slots(m, r)
                for s in range(nslots):
                    rows = pl.ds(r * 16, 16)
                    slots[m, s, rows, :] = (sums[s] + from_end[m, s, rows, :].astype(f32)).astype(bf16)
            send(slots.at[m], from_mid.at[m], group_send.at[1], mid_sem.at[m], mid_id)

        v = i - LAG_AVG

        @pl.when(jnp.logical_and(is_mid, jnp.logical_and(v >= 0, v < units)))
        def _():
            wait(from_mid.at[v], mid_sem.at[v])
            for r in range(quarter // 16):
                rows = pl.ds(r * 16, 16)
                for s in range(nslots):
                    total = slots[v, s, rows, :].astype(f32) + from_mid[v, s, rows, :].astype(f32)
                    avg[v, s, rows, :] = (table[64 + s] * total).astype(bf16)
            send(avg.at[v], from_end.at[v], group_send.at[3], end_sem.at[v], mate_id)
            send_back(v, avg)

        b = i - LAG_RET

        @pl.when(jnp.logical_and(jnp.logical_not(is_mid), jnp.logical_and(b >= 0, b < units)))
        def _():
            wait(from_end.at[b], end_sem.at[b])
            send_back(b, from_end)

        p = i - (units - 1)

        @pl.when(jnp.logical_and(p >= 0, p < 2 * NX))
        def _():
            @pl.when(p == 0)
            def _():
                loads[4].wait()

            here = pl.ds(pl.multiple_of(p * 2 * block, 2 * block), 2 * block)
            total = jnp.zeros((2 * block, pre_act.shape[1]), f32)
            for c in range(chunks):
                total += lax.dot_general(
                    gbuf[c, here, :], w_down[:, c * COLS:(c + 1) * COLS],
                    (((1,), (1,)), ((), ())), preferred_element_type=f32,
                )
            total = (total * slope[here, :]).astype(bf16)
            place_core, place_x = p // NX, lax.rem(p, NX)
            for half in range(2):
                rows = pl.ds(pl.multiple_of((half * 2 * NX + place_x * 2 + place_core) * block, block), block)
                pre[rows, :] = total[half * block:(half + 1) * block]
                pltpu.make_async_copy(pre.at[rows], pre_out.at[rows], store_sem.at[1]).start()

        return carry

    for c in range(AHEAD):
        send_own(c)
    loads[1].wait()
    lax.fori_loop(0, units + LAG_RET, tick, 0)

    wait(gbuf.at[:, pl.ds(0, block)], cot_send.at[0])
    wait(gbuf.at[:, pl.ds(0, 6 * block)], cot_send.at[1])
    wait(gbuf.at[:, pl.ds(0, 2 * NX * block)], cot_send.at[2])
    wait(raw, group_send.at[0])
    wait(slots, group_send.at[1])
    wait(raw, group_send.at[2])
    wait(raw, ret_sem.at[0])
    wait(raw.at[:, 0], store_sem.at[0])
    wait(pre, store_sem.at[1])

    @pl.when(is_mid)
    def _():
        wait(avg, group_send.at[3])


def fill_table(nslots, table, path, counts):
    one, zero = jnp.float32(1.0), jnp.float32(0.0)
    groups = range(NY * NZ)
    paths = [path[g] for g in groups]
    same = {}
    for g in groups:
        for h in range(g):
            same[g, h] = same[h, g] = jnp.where(paths[g] == paths[h], 1, 0)
    opened = jnp.int32(0)
    inverses = [zero] * nslots
    opens, ids = [], []
    for g in groups:
        count = counts[paths[g]]
        inverse = one
        for n in range(2, 9):
            inverse = jnp.where(count == n, jnp.float32(1.0 / n), inverse)
        earlier, spans = jnp.int32(0), jnp.int32(0)
        for h in groups:
            if h < g:
                earlier = jnp.maximum(earlier, same[g, h])
            if h % NZ != g % NZ:
                spans = jnp.maximum(spans, same[g, h])
        open_here = spans * (1 - earlier)
        slot = open_here * opened
        for h in range(g):
            slot += opens[h] * same[g, h] * ids[h]
        opens.append(open_here)
        ids.append(opened)
        for s in range(nslots):
            table[s * 16 + g] = jnp.where(spans * jnp.where(slot == s, 1, 0) == 1, one, zero)
            inverses[s] = jnp.where(open_here * jnp.where(opened == s, 1, 0) == 1, inverse, inverses[s])
        for k in range(NY):
            h = k * NZ + g % NZ
            local = (1 - spans) * (1 if h == g else same[g, h])
            table[80 + g * NY + k] = jnp.where(local == 1, inverse, zero)
        opened = opened + open_here
    for s in range(nslots):
        table[64 + s] = inverses[s]


def slots_needed(path_table):
    ids = jnp.arange(path_table.shape[0], dtype=jnp.int32)
    same = path_table[:, None] == path_table[None, :]
    spans = jnp.any(same & (ids[:, None] % NZ != ids[None, :] % NZ), axis=1)
    earlier = jnp.any(same & (ids[None, :] < ids[:, None]), axis=1)
    return jnp.sum((spans & ~earlier).astype(jnp.int32))


def finish(chunks, means, pre_in, grad_out, first_out, second_out, pre_out):
    f32 = jnp.float32
    for c in range(chunks):
        cols = slice(c * COLS, (c + 1) * COLS)
        grad_mean = means[chunks + 2 * c]
        grad_out[:, cols] = grad_mean
        first_out[:, cols] = 0.9 * means[c].astype(f32) + 0.1 * grad_mean.astype(f32)
        second_out[:, cols] = means[chunks + 2 * c + 1].astype(f32)
    pre_out[...] = pre_in[...]


def exchange(nslots, path_table, sharer_counts, pre_act, cotangent, w_down, first_moment, second_moment):
    f32, bf16 = jnp.float32, jnp.bfloat16
    block, width = cotangent.shape
    tokens, hidden = pre_act.shape
    chunks, quarter = width // COLS, hidden // NY
    units = 3 * chunks
    vmem, hbm = pltpu.VMEM, pl.BlockSpec(memory_space=pl.ANY)
    smem = pl.BlockSpec(memory_space=pltpu.SMEM)
    held = vmem((units, nslots, quarter, COLS), bf16)
    return pl.pallas_call(
        functools.partial(kernel, nslots, chunks, block, quarter, 1.0 / math.sqrt(tokens)),
        out_shape=(
            jax.ShapeDtypeStruct((units, hidden, COLS), bf16),
            jax.ShapeDtypeStruct((tokens, hidden), bf16),
        ),
        in_specs=[smem] * 2 + [hbm] * 5,
        out_specs=(hbm,) * 2,
        scratch_shapes=[
            pltpu.SMEM((144,), f32),
            vmem((tokens, hidden), bf16),
            vmem((block, width), bf16),
            vmem((hidden, width), bf16),
            vmem((hidden, width), f32),
            vmem((hidden, width), f32),
            vmem((chunks, tokens, COLS), bf16),
            vmem((hidden, tokens), bf16),
            vmem((tokens, hidden), f32),
            vmem((hidden, COLS), f32),
            vmem((units, hidden, COLS), bf16),
            vmem((units, 3, quarter, COLS), bf16),
            held,
            held,
            held,
            held,
            vmem((units, 4, quarter, COLS), bf16),
            vmem((tokens, hidden), bf16),
            pltpu.SemaphoreType.DMA((5,)),
            pltpu.SemaphoreType.DMA((2,)),
            pltpu.SemaphoreType.DMA((3,)),
            pltpu.SemaphoreType.DMA((4,)),
            pltpu.SemaphoreType.DMA((chunks,)),
            pltpu.SemaphoreType.DMA((chunks,)),
            pltpu.SemaphoreType.DMA((chunks,)),
            pltpu.SemaphoreType.DMA((units,)),
            pltpu.SemaphoreType.DMA((units,)),
            pltpu.SemaphoreType.DMA((units,)),
            pltpu.SemaphoreType.DMA((1,)),
        ],
        compiler_params=pltpu.CompilerParams(
            collective_id=nslots - FEWEST_SLOTS, has_side_effects=True, vmem_limit_bytes=60 * 2**20
        ),
        cost_estimate=pl.CostEstimate(
            flops=4 * tokens * hidden * width, bytes_accessed=13 * 2**20, transcendentals=2 * tokens * hidden
        ),
        name=f"routed_down_grad_{nslots}",
    )(path_table, sharer_counts, pre_act, cotangent, w_down, first_moment, second_moment)


def per_device(pre_act, cotangent, w_down, first_moment, second_moment, path_table, sharer_counts):
    f32, bf16 = jnp.float32, jnp.bfloat16
    tokens, hidden = pre_act.shape[1:]
    width = cotangent.shape[2]
    chunks = width // COLS
    units = 3 * chunks
    branches = [functools.partial(exchange, n) for n in range(FEWEST_SLOTS, MOST_SLOTS + 1)]
    index = jnp.clip(slots_needed(path_table) - FEWEST_SLOTS, 0, MOST_SLOTS - FEWEST_SLOTS)
    means, pre = lax.switch(
        index, branches, path_table, sharer_counts,
        pre_act[0], cotangent[0], w_down[0], first_moment[0], second_moment[0],
    )
    wide = pl.BlockSpec((hidden // STEPS, width), lambda c: (c, 0))
    tall = pl.BlockSpec((tokens // STEPS, hidden), lambda c: (c, 0))
    outs = pl.pallas_call(
        functools.partial(finish, chunks),
        grid=(STEPS,),
        out_shape=(
            jax.ShapeDtypeStruct((hidden, width), bf16),
            jax.ShapeDtypeStruct((hidden, width), f32),
            jax.ShapeDtypeStruct((hidden, width), f32),
            jax.ShapeDtypeStruct((tokens, hidden), bf16),
        ),
        in_specs=[pl.BlockSpec((units, hidden // STEPS, COLS), lambda c: (0, c, 0)), tall],
        out_specs=(wide, wide, wide, tall),
        compiler_params=pltpu.CompilerParams(vmem_limit_bytes=60 * 2**20),
        name="widen",
    )(means, pre)
    return tuple(out[None] for out in outs)


def solution(mesh):
    placed = (
        P("grp", None, "tp"),
        P("grp", "tp", None),
        P("grp", "tp", None),
        P("grp", "tp", None),
        P("grp", "tp", None),
        P(),
        P(),
    )
    return jax.shard_map(
        per_device,
        mesh=mesh,
        in_specs=placed,
        out_specs=(
            P("grp", "tp", None),
            P("grp", "tp", None),
            P("grp", "tp", None),
            P("grp", None, "tp"),
        ),
        check_vma=False,
    )
```

time: 135 us -> 99 us (0.73)
  Pallas kernels: 125 us -> 96 us
  local copies, waits for them, and re-layouts: 7.81 us -> 0 us
    pallas_call x1 -> x2, Pallas kernels: 125 us -> 96 us  [the longest x1 91.6 us: exchange(): pl.pallas_call(functools.partial(kernel, nslots, chunks, block, quarter,...]
    unnamed x10 -> x0, local copies, waits for them, and re-layouts: 7.73 us -> none
where the time goes in v2:
time: 99 us; the launch traced here: 98.8 us
  Pallas kernels  96 us (97%)
  other arithmetic  1.56 us (2%)
  between operations  1.3 us (1%)
    pallas_call x1, Pallas kernels, exchange(): pl.pallas_call(functools.partial(kernel, nslots, chunks, block, quarter,...  91.6 us
    pallas_call x1, Pallas kernels, per_device(): pl.pallas_call(functools.partial(finish, chunks), grid=(STEPS,), out_shap...  4.37 us

profile of v2, /device:TPU:6, one launch (start us, length us, event | category | flops | bytes accessed | tf_op | source)
XLA Modules:
  0.0 98.8 jit_solution(2494554846812488274)
XLA Ops:
  0.6 0.9 fusion
  1.6 0.6 fusion.2
  2.9 91.6 %conditional.1 = ((bf16[24,256,256]{2,1,0:T(8,128)(2,1)S(1)}, bf16[2048,256]{1,0:T(8,128)(2,1)})) conditional(s32[]{:T(128)} %clamp.3, (s32[16]{0:T(128)}, s32[16]{0:T(128)}, bf16[2048,256]{1,0:T(8,128)(2,1)}, bf16[128,2048]{1,0:T(8,128)(2,1)}, bf16[256,2048]{1,0:T(8,128)(2,1)}, /*index=5*/f32[256,2048]{1,0:T(8,128)}, ...), branch_computations={%region_3.4_spmd, %region_4.5_spmd, %region_5.6_spmd} | conditional | flops 4294967296 | bytes 13631496 | solution.py:405
  2.9 91.6 %routed_down_grad_2.1 = (bf16[24,256,256]{2,1,0:T(8,128)(2,1)S(1)}, bf16[2048,256]{1,0:T(8,128)(2,1)}) custom-call(s32[16]{0:T(128)} %get-tuple-element.42.path, s32[16]{0:T(128)} %get-tuple-element.43.counts, bf16[2048,256]{1,0:T(8,128)(2,1)} %get-tuple-element.44.pre_act_in, bf16[128,2048]{1,0:T(8,128)(2,1)} %get-tuple-element.45.cot_in, ...), custom_call_target="tpu_custom_call" | custom-call | flops 4294967296 | bytes 13631488 | tf_op jit(solution)/shard_map/cond/branch_0_fun/routed_down_grad_2/pallas_call | solution.py:348
  94.5 4.4 %widen.1 = (bf16[256,2048]{1,0:T(8,128)(2,1)}, f32[256,2048]{1,0:T(8,128)}, f32[256,2048]{1,0:T(8,128)}, bf16[2048,256]{1,0:T(8,128)(2,1)}) custom-call(bf16[24,256,256]{2,1,0:T(8,128)(2,1)S(1)} %get-tuple-element.73.means, bf16[2048,256]{1,0:T(8,128)(2,1)} %get-tuple-element.74.pre_in), custom_call_target="tpu_custom_call" | custom-call | tf_op jit(solution)/shard_map/widen/pallas_call | solution.py:411
  (1 shorter events, 0.0 us)

commit v3 on v2

--- a/solution.py
+++ b/solution.py
@@ -9,16 +9,16 @@
 from jax.sharding import PartitionSpec as P
 
 MESH = pl.DeviceIdType.MESH
-COLS = 256
+COLS = 128
 NY = 4
 NZ = 4
 NX = 4
 FEWEST_SLOTS, MOST_SLOTS = 2, 4
-LAG_END, LAG_MID, LAG_AVG, LAG_RET = 3, 6, 9, 12
-
-B_AT, C_AT = 2, 7
-AHEAD = 2
-STEPS = 4
+LAG_END, LAG_MID, LAG_AVG, LAG_RET = 7, 11, 15, 19
+
+B_AT, C_AT = 10, 15
+AHEAD = 4
+STEPS = 2
 
 INV_ROOT_TWO = 1.0 / math.sqrt(2.0)
 INV_ROOT_TAU = 1.0 / math.sqrt(2.0 * math.pi)
@@ -137,15 +137,16 @@
         def _():
             mine[i] = first[:, columns(i)].astype(bf16)
             send_raw(i)
-            place_core, place_x = i // NX, lax.rem(i, NX)
 
             @pl.when(i == 0)
             def _():
                 loads[2].wait()
 
-            for half in range(2):
-                rows = pl.ds(pl.multiple_of((half * 2 * NX + place_x * 2 + place_core) * block, block), block)
-                put = pl.ds(pl.multiple_of((i * 2 + half) * block, block), block)
+            for k in range(4 * NX // chunks):
+                place = i * (4 * NX // chunks) + k
+                owner = lax.rem(place, 2) * 2 * NX + lax.rem(place // 2, NX) * 2 + place // (2 * NX)
+                rows = pl.ds(pl.multiple_of(owner * block, block), block)
+                put = pl.ds(pl.multiple_of(place * block, block), block)
                 inputs = pre_act[rows, :].astype(f32)
                 cdf = 0.5 * (1.0 + lax.erf(inputs * INV_ROOT_TWO))
                 slope[put, :] = cdf + inputs * jnp.exp(-0.5 * inputs * inputs) * INV_ROOT_TAU
@@ -260,7 +261,7 @@
     for c in range(AHEAD):
         send_own(c)
     loads[1].wait()
-    lax.fori_loop(0, units + LAG_RET, tick, 0)
+    lax.fori_loop(0, units + max(LAG_RET, 2 * NX - 1), tick, 0)
 
     wait(gbuf.at[:, pl.ds(0, block)], cot_send.at[0])
     wait(gbuf.at[:, pl.ds(0, 6 * block)], cot_send.at[1])

time: 99 us -> 93.5 us (0.944); the launches traced: 98.8 us -> 92.3 us
  Pallas kernels: 96 us -> 89.4 us
    pallas_call x1, Pallas kernels: 91.6 us -> 85.2 us  [exchange(): pl.pallas_call(functools.partial(kernel, nslots, chunks, block, quarter,...]
where the time goes in v3:
time: 93.5 us; the launch traced here: 92.3 us
  Pallas kernels  89.4 us (96%)
  other arithmetic  1.56 us (2%)
  between operations  1.3 us (1%)
    pallas_call x1, Pallas kernels, exchange(): pl.pallas_call(functools.partial(kernel, nslots, chunks, block, quarter,...  85.2 us
    pallas_call x1, Pallas kernels, per_device(): pl.pallas_call(functools.partial(finish, chunks), grid=(STEPS,), out_shap...  4.19 us

profile of v3, /device:TPU:6, one launch (start us, length us, event | category | flops | bytes accessed | tf_op | source)
XLA Modules:
  0.0 92.3 jit_solution(7838064034067642241)
XLA Ops:
  0.6 0.9 fusion
  1.6 0.6 fusion.2
  2.9 85.2 %conditional.1 = ((bf16[48,256,128]{2,1,0:T(8,128)(2,1)S(1)}, bf16[2048,256]{1,0:T(8,128)(2,1)})) conditional(s32[]{:T(128)} %clamp.3, (s32[16]{0:T(128)}, s32[16]{0:T(128)}, bf16[2048,256]{1,0:T(8,128)(2,1)}, bf16[128,2048]{1,0:T(8,128)(2,1)}, bf16[256,2048]{1,0:T(8,128)(2,1)}, /*index=5*/f32[256,2048]{1,0:T(8,128)}, ...), branch_computations={%region_3.4_spmd, %region_4.5_spmd, %region_5.6_spmd} | conditional | flops 4294967296 | bytes 13631496 | solution.py:406
  2.9 85.2 %routed_down_grad_2.1 = (bf16[48,256,128]{2,1,0:T(8,128)(2,1)S(1)}, bf16[2048,256]{1,0:T(8,128)(2,1)}) custom-call(s32[16]{0:T(128)} %get-tuple-element.42.path, s32[16]{0:T(128)} %get-tuple-element.43.counts, bf16[2048,256]{1,0:T(8,128)(2,1)} %get-tuple-element.44.pre_act_in, bf16[128,2048]{1,0:T(8,128)(2,1)} %get-tuple-element.45.cot_in, ...), custom_call_target="tpu_custom_call" | custom-call | flops 4294967296 | bytes 13631488 | tf_op jit(solution)/shard_map/cond/branch_0_fun/routed_down_grad_2/pallas_call | solution.py:349
  88.1 4.2 %widen.1 = (bf16[256,2048]{1,0:T(8,128)(2,1)}, f32[256,2048]{1,0:T(8,128)}, f32[256,2048]{1,0:T(8,128)}, bf16[2048,256]{1,0:T(8,128)(2,1)}) custom-call(bf16[48,256,128]{2,1,0:T(8,128)(2,1)S(1)} %get-tuple-element.73.means, bf16[2048,256]{1,0:T(8,128)(2,1)} %get-tuple-element.74.pre_in), custom_call_target="tpu_custom_call" | custom-call | tf_op jit(solution)/shard_map/widen/pallas_call | solution.py:412
  (1 shorter events, 0.0 us)

commit v4 on v3

--- a/solution.py
+++ b/solution.py
@@ -18,7 +18,7 @@
 
 B_AT, C_AT = 10, 15
 AHEAD = 4
-STEPS = 2
+STEPS = 4
 
 INV_ROOT_TWO = 1.0 / math.sqrt(2.0)
 INV_ROOT_TAU = 1.0 / math.sqrt(2.0 * math.pi)
@@ -234,7 +234,7 @@
             wait(from_end.at[b], end_sem.at[b])
             send_back(b, from_end)
 
-        p = i - (units - 1)
+        p = i - (units + LAG_RET - 2 * NX)
 
         @pl.when(jnp.logical_and(p >= 0, p < 2 * NX))
         def _():
@@ -261,7 +261,7 @@
     for c in range(AHEAD):
         send_own(c)
     loads[1].wait()
-    lax.fori_loop(0, units + max(LAG_RET, 2 * NX - 1), tick, 0)
+    lax.fori_loop(0, units + LAG_RET, tick, 0)
 
     wait(gbuf.at[:, pl.ds(0, block)], cot_send.at[0])
     wait(gbuf.at[:, pl.ds(0, 6 * block)], cot_send.at[1])
@@ -326,15 +326,27 @@
     return jnp.sum((spans & ~earlier).astype(jnp.int32))
 
 
-def finish(chunks, means, pre_in, grad_out, first_out, second_out, pre_out):
+def finish(chunks, means, pre_in, grad_out, first_out, second_out, pre_out, grad, first, second, pre, sem):
     f32 = jnp.float32
-    for c in range(chunks):
-        cols = slice(c * COLS, (c + 1) * COLS)
-        grad_mean = means[chunks + 2 * c]
-        grad_out[:, cols] = grad_mean
-        first_out[:, cols] = 0.9 * means[c].astype(f32) + 0.1 * grad_mean.astype(f32)
-        second_out[:, cols] = means[chunks + 2 * c + 1].astype(f32)
-    pre_out[...] = pre_in[...]
+    load = pltpu.make_async_copy(pre_in, pre, sem.at[3])
+    store = pltpu.make_async_copy(pre, pre_out, sem.at[4])
+    load.start()
+    depth = grad.shape[0] // STEPS
+    for r in range(STEPS):
+        rows = slice(r * depth, (r + 1) * depth)
+        for c in range(chunks):
+            cols = slice(c * COLS, (c + 1) * COLS)
+            grad_mean = means[chunks + 2 * c, rows, :]
+            grad[rows, cols] = grad_mean
+            first[rows, cols] = 0.9 * means[c, rows, :].astype(f32) + 0.1 * grad_mean.astype(f32)
+            second[rows, cols] = means[chunks + 2 * c + 1, rows, :].astype(f32)
+        for k, (held, out) in enumerate(((grad, grad_out), (first, first_out), (second, second_out))):
+            pltpu.make_async_copy(held.at[rows], out.at[rows], sem.at[k]).start()
+    load.wait()
+    store.start()
+    for k, held in enumerate((grad, first, second)):
+        pltpu.make_async_copy(held, held, sem.at[k]).wait()
+    store.wait()
 
 
 def exchange(nslots, path_table, sharer_counts, pre_act, cotangent, w_down, first_moment, second_moment):
@@ -400,26 +412,30 @@
     tokens, hidden = pre_act.shape[1:]
     width = cotangent.shape[2]
     chunks = width // COLS
-    units = 3 * chunks
     branches = [functools.partial(exchange, n) for n in range(FEWEST_SLOTS, MOST_SLOTS + 1)]
     index = jnp.clip(slots_needed(path_table) - FEWEST_SLOTS, 0, MOST_SLOTS - FEWEST_SLOTS)
     means, pre = lax.switch(
         index, branches, path_table, sharer_counts,
         pre_act[0], cotangent[0], w_down[0], first_moment[0], second_moment[0],
     )
-    wide = pl.BlockSpec((hidden // STEPS, width), lambda c: (c, 0))
-    tall = pl.BlockSpec((tokens // STEPS, hidden), lambda c: (c, 0))
+    hbm = pl.BlockSpec(memory_space=pl.ANY)
     outs = pl.pallas_call(
         functools.partial(finish, chunks),
-        grid=(STEPS,),
         out_shape=(
             jax.ShapeDtypeStruct((hidden, width), bf16),
             jax.ShapeDtypeStruct((hidden, width), f32),
             jax.ShapeDtypeStruct((hidden, width), f32),
             jax.ShapeDtypeStruct((tokens, hidden), bf16),
         ),
-        in_specs=[pl.BlockSpec((units, hidden // STEPS, COLS), lambda c: (0, c, 0)), tall],
-        out_specs=(wide, wide, wide, tall),
+        in_specs=[pl.BlockSpec(memory_space=pltpu.VMEM), hbm],
+        out_specs=(hbm,) * 4,
+        scratch_shapes=[
+            pltpu.VMEM((hidden, width), bf16),
+            pltpu.VMEM((hidden, width), f32),
+            pltpu.VMEM((hidden, width), f32),
+            pltpu.VMEM((tokens, hidden), bf16),
+            pltpu.SemaphoreType.DMA((5,)),
+        ],
         compiler_params=pltpu.CompilerParams(vmem_limit_bytes=60 * 2**20),
         name="widen",
     )(means, pre)

time: 93.5 us -> 92.1 us (0.985)
  Pallas kernels: 89.4 us -> 88 us
    pallas_call x1, Pallas kernels: 4.19 us -> 2.81 us  [per_device(): pl.pallas_call(functools.partial(finish, chunks), out_shape=(jax.ShapeDty...]
where the time goes in v4:
time: 92.1 us; the launch traced here: 90.9 us
  Pallas kernels  88 us (96%)
  other arithmetic  1.56 us (2%)
  between operations  1.3 us (1%)
    pallas_call x1, Pallas kernels, exchange(): pl.pallas_call(functools.partial(kernel, nslots, chunks, block, quarter,...  85.2 us
    pallas_call x1, Pallas kernels, per_device(): pl.pallas_call(functools.partial(finish, chunks), out_shape=(jax.ShapeDty...  2.81 us

profile of v4, /device:TPU:6, one launch (start us, length us, event | category | flops | bytes accessed | tf_op | source)
XLA Modules:
  0.0 90.9 jit_solution(1420562552502118737)
XLA Ops:
  0.6 0.9 %fusion = (pred[16]{0:T(512)(128)(4,1)S(1)}, pred[16]{0:T(512)(128)(4,1)S(1)}) fusion(s32[16]{0:T(128)} %param.15, s32[16]{0:T(128)S(1)} %and_select_fusion), kind=kLoop, calls=%fused_computation.3 | loop fusion | flops 1760 | bytes 160 | tf_op jit(solution)/shard_map/reduce_or | solution.py:325
  1.6 0.6 fusion.2
  2.9 85.2 %conditional.1 = ((bf16[48,256,128]{2,1,0:T(8,128)(2,1)S(1)}, bf16[2048,256]{1,0:T(8,128)(2,1)})) conditional(s32[]{:T(128)} %clamp.3, (s32[16]{0:T(128)}, s32[16]{0:T(128)}, bf16[2048,256]{1,0:T(8,128)(2,1)}, bf16[128,2048]{1,0:T(8,128)(2,1)}, bf16[256,2048]{1,0:T(8,128)(2,1)}, /*index=5*/f32[256,2048]{1,0:T(8,128)}, ...), branch_computations={%region_3.4_spmd, %region_4.5_spmd, %region_5.6_spmd} | conditional | flops 4294967296 | bytes 13631496 | solution.py:417
  2.9 85.2 %routed_down_grad_2.1 = (bf16[48,256,128]{2,1,0:T(8,128)(2,1)S(1)}, bf16[2048,256]{1,0:T(8,128)(2,1)}) custom-call(s32[16]{0:T(128)} %get-tuple-element.42.path, s32[16]{0:T(128)} %get-tuple-element.43.counts, bf16[2048,256]{1,0:T(8,128)(2,1)} %get-tuple-element.44.pre_act_in, bf16[128,2048]{1,0:T(8,128)(2,1)} %get-tuple-element.45.cot_in, ...), custom_call_target="tpu_custom_call" | custom-call | flops 4294967296 | bytes 13631488 | tf_op jit(solution)/shard_map/cond/branch_0_fun/routed_down_grad_2/pallas_call | solution.py:361
  88.1 2.8 %widen.1 = (bf16[256,2048]{1,0:T(8,128)(2,1)}, f32[256,2048]{1,0:T(8,128)}, f32[256,2048]{1,0:T(8,128)}, bf16[2048,256]{1,0:T(8,128)(2,1)}) custom-call(bf16[48,256,128]{2,1,0:T(8,128)(2,1)S(1)} %get-tuple-element.73.means, bf16[2048,256]{1,0:T(8,128)(2,1)} %get-tuple-element.74.pre_in), custom_call_target="tpu_custom_call" | custom-call | tf_op jit(solution)/shard_map/widen/pallas_call | solution.py:422
  (1 shorter events, 0.0 us)
